TPU v7x, 128 devices: a whole 4x4x4 slice. The times are simulated.
128 devices in a mesh: gx: 8 (over x, z_hi), gy: 4 (over z_lo, core), gz: 4 (over y).
Axes of the slice: x: 4, y: 4, z: 4 (z_hi: 2, z_lo: 2; z = z_hi * 2 + z_lo), core: 2. Of those that a mesh axis runs over, the one named last changes fastest.
Arguments:
- rhs_field: float32 [192, 128, 1024], P('gz', 'gy', 'gx'), may hold values from -24 to 24
- stiffness: float32 [192, 128, 1024], P('gz', 'gy', 'gx'), may hold values from 0.03 to 0.3
Outputs:
- solution: float32 [192, 128, 1024], P('gz', 'gy', 'gx')
- residual: float32 [192, 128, 1024], P('gz', 'gy', 'gx')
All inputs are finite; a program needn't handle non-finite values.
Results may differ from a plain program's by a relative error of at most 0.0015.
Values sent between devices are 32-bit elements; how exact they have to be, the bound alone decides.
No kernel may reach another device: no remote copies, remote signals or barrier semaphores. Data moves between devices by JAX's collectives and lax.ppermute only.
A program may use at most 128 MiB of HBM per device.

v0:
```python
import jax
import jax.numpy as jnp
from jax import lax
from jax.sharding import PartitionSpec as P

OV = 4
ITERS = 3


mass_term = 1e-05
split_term = 0.5
bend_mean = 0.1
highest = lax.Precision.HIGHEST


def extended_2(block, sides, width):
    for axis, dim in sides:
        count = lax.axis_size(axis)
        forward = [(i, i + 1) for i in range(count - 1)]
        forward.append((count - 1, 0))
        backward = [(target, source) for source, target in forward]
        low = lax.ppermute(
            lax.slice_in_dim(block, block.shape[dim] - width, None, axis=dim), axis, forward
        )
        high = lax.ppermute(lax.slice_in_dim(block, 0, width, axis=dim), axis, backward)
        block = jnp.concatenate([low, block, high], axis=dim)
    return block


def sine_table(length):
    places = jnp.arange(1, length + 1, dtype=jnp.float32)
    factor = jnp.sqrt(2.0 / (length + 1.0))
    return factor * jnp.sin(jnp.pi * places[:, None] * places[None, :] / (length + 1.0))


def eigen_line(length):
    places = jnp.arange(1, length + 1, dtype=jnp.float32)
    return 2.0 - 2.0 * jnp.cos(jnp.pi * places / (length + 1.0))


def transform(values, tables):
    depth_table, row_table, column_table = tables
    values = jnp.einsum("zyx,xc->zyc", values, column_table, precision=highest)
    values = jnp.einsum("zyx,yb->zbx", values, row_table, precision=highest)
    return jnp.einsum("zyx,za->ayx", values, depth_table, precision=highest)


def local_solve(values):
    depth_len, row_len, column_len = values.shape
    tables = (sine_table(depth_len), sine_table(row_len), sine_table(column_len))
    spectrum = (
        eigen_line(depth_len)[:, None, None]
        + eigen_line(row_len)[None, :, None]
        + eigen_line(column_len)[None, None, :]
    )
    inverse = 1.0 / (mass_term + bend_mean * spectrum * spectrum + split_term * spectrum)
    return transform(transform(values, tables) * inverse, tables)


def crop(values, margin):
    if margin == 0:
        return values
    return values[margin:-margin, margin:-margin, margin:-margin]


def laplace(values):
    centre = values[1:-1, 1:-1, 1:-1]
    beside = values[2:, 1:-1, 1:-1] + values[:-2, 1:-1, 1:-1]
    beside = beside + values[1:-1, 2:, 1:-1] + values[1:-1, :-2, 1:-1]
    beside = beside + values[1:-1, 1:-1, 2:] + values[1:-1, 1:-1, :-2]
    return 6.0 * centre - beside


def operate(values, value_margin, stiffness, stiff_margin, out_margin):
    widened = crop(values, value_margin - out_margin - 2)
    flux = laplace(widened)
    weighted = crop(stiffness, stiff_margin - out_margin - 1) * flux
    return mass_term * crop(widened, 2) + laplace(weighted) + split_term * crop(flux, 1)


def edges(values, rim_width, axis_dim):
    extent = values.shape[axis_dim]
    below_part = lax.slice_in_dim(values, 0, rim_width, axis=axis_dim)
    above_part = lax.slice_in_dim(values, extent - rim_width, extent, axis=axis_dim)
    return jnp.concatenate([below_part, above_part], axis=axis_dim)


def place(values, padded, rim_width, margin, axis_dim):
    extent = values.shape[axis_dim]
    core_len = extent - 2 * OV
    length = core_len + 2 * margin
    owned = lax.slice_in_dim(values, OV - margin, OV - margin + length, axis=axis_dim)
    below_pad = lax.slice_in_dim(padded, 0, rim_width, axis=axis_dim)
    above_pad = lax.slice_in_dim(padded, 3 * rim_width, 4 * rim_width, axis=axis_dim)
    first_cut = [slice(None)] * 3
    first_cut[axis_dim] = slice(0, rim_width)
    last_cut = [slice(None)] * 3
    last_cut[axis_dim] = slice(length - rim_width, length)
    return owned.at[tuple(first_cut)].add(below_pad).at[tuple(last_cut)].add(above_pad)


def fold(extended, margin):
    rim_width = OV + margin
    padded = extended_2(edges(extended, rim_width, 0), (("gz", 0),), rim_width)
    extended = place(extended, padded, rim_width, margin, 0)
    padded = extended_2(edges(extended, rim_width, 1), (("gy", 1),), rim_width)
    extended = place(extended, padded, rim_width, margin, 1)
    padded = extended_2(edges(extended, rim_width, 2), (("gx", 2),), rim_width)
    return place(extended, padded, rim_width, margin, 2)


def per_device(rhs_field, stiffness):
    stiff_wide = extended_2(stiffness, (("gx", 2), ("gy", 1), ("gz", 0)), 1)
    stiff_margin = 1
    residual = rhs_field
    res_margin = 0
    keep_margin = 2

    def precondition(current_res):
        extended = extended_2(current_res, (("gx", 2), ("gy", 1), ("gz", 0)), OV)
        return fold(local_solve(extended), keep_margin)

    def residual_dot(current_res, smoothed):
        local_sum = jnp.sum(crop(current_res, res_margin) * crop(smoothed, keep_margin))
        return lax.psum(local_sum, ("gx", "gy", "gz"))

    solution = jnp.zeros(rhs_field.shape, jnp.float32)
    smoothed = precondition(residual)
    direction = smoothed
    current = residual_dot(residual, smoothed)
    for turn_index in range(ITERS):
        applied = operate(direction, keep_margin, stiff_wide, stiff_margin, res_margin)
        direction_core = crop(direction, keep_margin)
        bending = lax.psum(jnp.sum(direction_core * crop(applied, res_margin)), ("gx", "gy", "gz"))
        step_size = current / bending
        solution = solution + step_size * direction_core
        residual = residual - step_size * applied
        if turn_index + 1 < ITERS:
            smoothed = precondition(residual)
            following = residual_dot(residual, smoothed)
            direction = smoothed + following / current * direction
            current = following
    return (solution, crop(residual, res_margin))


def solution(mesh):
    in_specs = (P("gz", "gy", "gx"), P("gz", "gy", "gx"))
    out_specs = (P("gz", "gy", "gx"), P("gz", "gy", "gx"))
    return jax.shard_map(
        per_device, mesh=mesh, in_specs=in_specs, out_specs=out_specs, check_vma=False
    )
```

profile of v0, /device:TPU:0, one launch (start us, length us, event | category | flops | bytes accessed | tf_op | source)
XLA Modules:
  0.0 753.4 jit_solution(3096796113450964716)
XLA Ops:
  2.9 6.2 collective-permute-start.1
  9.9 7.6 %collective-permute-done = f32[48,32,4]{0,1,2:T(8,128)S(1)} collective-permute-done((f32[48,32,4]{0,1,2:T(8,128)S(1)}, f32[48,32,4]{0,1,2:T(8,128)S(1)}, u32[]{:S(2)}, u32[]{:S(2)}) %collective-permute-start) | collective-permute-done | bytes 24608 | tf_op jit(solution)/shard_map/ppermute | solution.py:22
  21.2 4.1 collective-permute-done.2
  29.0 4.6 collective-permute-done.4
  34.3 3.1 fusion.3
  39.6 2.9 fusion.27
  42.5 3.3 fusion.40
  48.5 2.9 fusion.25
  56.3 6.1 collective-permute-done.6
  62.4 3.7 scatter-add.60
  67.3 3.8 scatter-add.61
  74.3 5.7 collective-permute-start.13
  85.8 3.7 collective-permute-done.9
  97.2 3.0 collective-permute-start.17
  102.5 4.1 collective-permute-start.11
  110.9 12.5 %scatter-add.66 = f32[52,36,132]{2,0,1:T(8,128)S(1)} dynamic-update-slice(f32[52,36,132]{2,0,1:T(8,128)S(1)} %slice.877, f32[52,36,6]{2,0,1:T(8,128)} %slice_add_fusion.20, s32[]{:T(128)} %constant.451.clone.1, s32[]{:T(128)} %constant.451.clone.1, s32[]{:T(128)} %constant.451.clone.1) | dynamic-update-slice | bytes 89860 | tf_op jit(solution)/shard_map/scatter-add | solution.py:99
  128.3 17.7 %scatter-add.69 = f32[52,36,132]{2,0,1:T(8,128)S(1)} dynamic-update-slice(f32[52,36,132]{2,0,1:T(8,128)S(1)} %scatter-add.66, f32[52,36,6]{2,0,1:T(8,128)} %slice_add_fusion.19, s32[]{:T(128)} %constant.451.clone.1, s32[]{:T(128)} %constant.451.clone.1, s32[]{:T(128)} %constant.454.clone.1) | dynamic-update-slice | bytes 89860 | tf_op jit(solution)/shard_map/scatter-add | solution.py:99
  146.1 5.9 fusion.213
  152.0 3.4 multiply_reduce_fusion.2
  155.4 63.0 %all-reduce = (f32[]{:T(128)}, f32[]{:T(128)}) all-reduce(f32[]{:T(128)} %get-tuple-element.223, f32[]{:T(128)} %get-tuple-element.222), channel_id=1, replica_groups=mesh['gx'=8,'gy'=4,'gz'=4] {'gx','gy','gz'}, use_global_device_ids=true, to_apply=%region_1.0 | all-reduce | flops 2 | bytes 16 | tf_op jit(solution)/shard_map/psum | solution.py:125
  228.8 2.9 collective-permute-start.19
  239.4 3.7 collective-permute-done.20
  246.8 4.9 collective-permute-done.22
  252.5 3.0 fusion.37
  257.7 2.9 fusion.23
  260.6 3.3 fusion.35
  266.3 2.9 fusion.21
  271.7 3.2 collective-permute-start.25
  274.9 6.3 collective-permute-done.24
  281.2 3.7 scatter-add.70
  286.2 3.7 scatter-add.71
  294.7 4.0 collective-permute-done.26
  306.9 3.5 slice.910
  312.1 3.6 collective-permute-start.29
  320.8 6.3 scatter-add.76
  328.6 3.2 slice_add_fusion.17
  331.8 9.6 %scatter-add.79 = f32[52,36,132]{2,0,1:T(8,128)} dynamic-update-slice(f32[52,36,132]{2,0,1:T(8,128)} %scatter-add.76, f32[52,36,6]{2,0,1:T(8,128)} %slice_add_fusion.17, s32[]{:T(128)} %constant.451.clone.1, s32[]{:T(128)} %constant.451.clone.1, s32[]{:T(128)} %constant.454.clone.1) | dynamic-update-slice | bytes 89860 | tf_op jit(solution)/shard_map/scatter-add | solution.py:99
  343.9 64.2 %psum.44 = f32[]{:T(128)} all-reduce(f32[]{:T(128)} %fusion.55), channel_id=1, replica_groups=mesh['gx'=8,'gy'=4,'gz'=4] {'gx','gy','gz'}, use_global_device_ids=true, to_apply=%region_5.0 | all-reduce | flops 1 | bytes 8 | tf_op jit(solution)/shard_map/psum | solution.py:125
  411.6 4.7 fusion.212
  416.3 3.3 multiply_reduce_fusion.1
  419.6 63.8 %psum.45 = f32[]{:T(128)} all-reduce(f32[]{:T(128)} %get-tuple-element.230), channel_id=1, replica_groups=mesh['gx'=8,'gy'=4,'gz'=4] {'gx','gy','gz'}, use_global_device_ids=true, to_apply=%region_7.0 | all-reduce | flops 1 | bytes 8 | tf_op jit(solution)/shard_map/psum | solution.py:134
  492.2 4.0 collective-permute-start.31
  502.7 5.3 collective-permute-done.32
  508.4 3.6 collective-permute-start.35
  512.0 3.8 collective-permute-done.34
  516.6 3.0 fusion.32
  521.8 2.9 fusion.19
  524.7 3.3 fusion.30
  530.4 2.9 fusion.17
  536.1 2.9 collective-permute-start.37
  539.0 5.3 collective-permute-done.36
  544.3 3.7 scatter-add.80
  549.3 3.7 scatter-add.81
  557.7 4.2 collective-permute-done.38
  570.4 3.5 slice.944
  575.6 3.3 collective-permute-start.41
  581.3 2.9 slice_add_fusion.16
  584.2 6.4 scatter-add.86
  592.1 3.2 slice_add_fusion.15
  595.3 9.6 %scatter-add.89 = f32[52,36,132]{2,0,1:T(8,128)} dynamic-update-slice(f32[52,36,132]{2,0,1:T(8,128)} %scatter-add.86, f32[52,36,6]{2,0,1:T(8,128)} %slice_add_fusion.15, s32[]{:T(128)} %constant.451.clone.1, s32[]{:T(128)} %constant.451.clone.1, s32[]{:T(128)} %constant.454.clone.1) | dynamic-update-slice | bytes 89860 | tf_op jit(solution)/shard_map/scatter-add | solution.py:99
  607.4 64.8 %psum.46 = f32[]{:T(128)} all-reduce(f32[]{:T(128)} %fusion.51), channel_id=1, replica_groups=mesh['gx'=8,'gy'=4,'gz'=4] {'gx','gy','gz'}, use_global_device_ids=true, to_apply=%region_9.0 | all-reduce | flops 1 | bytes 8 | tf_op jit(solution)/shard_map/psum | solution.py:125
  676.3 4.7 fusion.211
  681.1 3.2 multiply_reduce_fusion
  684.2 62.4 %psum.47 = f32[]{:T(128)} all-reduce(f32[]{:T(128)} %get-tuple-element.226), channel_id=1, replica_groups=mesh['gx'=8,'gy'=4,'gz'=4] {'gx','gy','gz'}, use_global_device_ids=true, to_apply=%region_11.0 | all-reduce | flops 1 | bytes 8 | tf_op jit(solution)/shard_map/psum | solution.py:134
  (207 shorter events, 158.3 us)
Async XLA Ops:
  2.4 16.6 %copy-start.12 = (f32[48,32,128]{2,1,0:T(8,128)S(1)}, f32[48,32,128]{2,1,0:T(8,128)}, u32[]{:S(2)}) copy-start(f32[48,32,128]{2,1,0:T(8,128)} %param.38) | copy-start | bytes 2359300
  2.9 15.4 %collective-permute-start.1 = (f32[48,32,4]{0,1,2:T(8,128)S(1)}, f32[48,32,4]{0,1,2:T(8,128)S(1)}, u32[]{:S(2)}, u32[]{:S(2)}) collective-permute-start(f32[48,32,4]{0,1,2:T(8,128)S(1)} %copy.56), channel_id=1, source_target_pairs={{16,0},{32,16},{48,32},{64,48},{80,64},{96,80},{112,96},{0,112},{1... | collective-permute-start | bytes 73736 | tf_op jit(solution)/shard_map/ppermute | solution.py:25
  9.6 7.9 %collective-permute-start = (f32[48,32,4]{0,1,2:T(8,128)S(1)}, f32[48,32,4]{0,1,2:T(8,128)S(1)}, u32[]{:S(2)}, u32[]{:S(2)}) collective-permute-start(f32[48,32,4]{0,1,2:T(8,128)S(1)} %copy.55), channel_id=1, source_target_pairs={{0,16},{16,32},{32,48},{48,64},{64,80},{80,96},{96,112},{112,0},{1... | collective-permute-start | bytes 73736 | tf_op jit(solution)/shard_map/ppermute | solution.py:22
  19.4 5.9 collective-permute-start.2
  19.5 5.8 collective-permute-start.3
  25.5 8.1 %collective-permute-start.4 = (f32[4,40,136]{2,1,0:T(8,128)S(1)}, f32[4,40,136]{2,1,0:T(8,128)S(1)}, u32[]{:S(2)}, u32[]{:S(2)}) collective-permute-start(f32[4,40,136]{2,1,0:T(8,128)S(1)} %get-tuple-element.241), channel_id=1, source_target_pairs={{0,1},{1,2},{2,3},{3,0},{4,5},{5,6},{6,7},{7,4},{8,9},{9,10},{10,1... | collective-permute-start | bytes 261128 | tf_op jit(solution)/shard_map/ppermute | solution.py:22
  27.2 7.2 collective-permute-start.5
  51.5 10.9 %collective-permute-start.6 = (f32[6,40,136]{2,0,1:T(8,128)S(1)}, f32[6,40,136]{2,0,1:T(8,128)S(1)}, u32[]{:S(2)}, u32[]{:S(2)}) collective-permute-start(f32[6,40,136]{2,0,1:T(8,128)S(1)} %get-tuple-element.264), channel_id=1, source_target_pairs={{0,1},{1,2},{2,3},{3,0},{4,5},{5,6},{6,7},{7,4},{8,9},{9,10},{10,1... | collective-permute-start | bytes 391688 | tf_op jit(solution)/shard_map/ppermute | solution.py:22
  54.6 18.3 %copy-start.23 = (f32[48,32,128]{2,1,0:T(8,128)S(1)}, f32[48,32,128]{2,1,0:T(8,128)}, u32[]{:S(2)}) copy-start(f32[48,32,128]{2,1,0:T(8,128)} %param.39) | copy-start | bytes 2359300
  54.6 11.5 %collective-permute-start.7 = (f32[6,40,136]{2,0,1:T(8,128)S(1)}, f32[6,40,136]{2,0,1:T(8,128)S(1)}, u32[]{:S(2)}, u32[]{:S(2)}) collective-permute-start(f32[6,40,136]{2,0,1:T(8,128)S(1)} %get-tuple-element.263), channel_id=1, source_target_pairs={{1,0},{2,1},{3,2},{0,3},{5,4},{6,5},{7,6},{4,7},{9,8},{10,9},{11,1... | collective-permute-start | bytes 391688 | tf_op jit(solution)/shard_map/ppermute | solution.py:25
  73.0 11.8 %collective-permute-start.8 = (f32[52,6,136]{2,0,1:T(8,128)}, f32[52,6,136]{2,0,1:T(8,128)}, u32[]{:S(2)}, u32[]{:S(2)}) collective-permute-start(f32[52,6,136]{2,0,1:T(8,128)} %get-tuple-element.262), channel_id=1, source_target_pairs={{0,4},{4,8},{8,12},{12,0},{1,5},{5,9},{9,13},{13,1},{2,6},{6,10},{... | collective-permute-start | bytes 509192 | tf_op jit(solution)/shard_map/ppermute | solution.py:22
  73.7 7.4 collective-permute-start.12
  74.3 7.2 collective-permute-start.13
  80.4 65.7 %copy-start.3 = (f32[48,32,128]{2,0,1:T(8,128)}, f32[48,32,128]{2,0,1:T(8,128)S(1)}, u32[]{:S(2)}) copy-start(f32[48,32,128]{2,0,1:T(8,128)S(1)} %copy.23) | copy-start | bytes 2359300
  81.5 15.0 %copy-start.6 = (f32[48,32,1]{2,0,1:T(8,128)}, f32[48,32,1]{2,0,1:T(8,128)S(1)}, u32[]{:S(2)}) copy-start(f32[48,32,1]{2,0,1:T(8,128)S(1)} %copy.22) | copy-start | bytes 18436
  81.8 14.7 %copy-start.9 = (f32[48,32,1]{2,0,1:T(8,128)}, f32[48,32,1]{2,0,1:T(8,128)S(1)}, u32[]{:S(2)}) copy-start(f32[48,32,1]{2,0,1:T(8,128)S(1)} %copy.24) | copy-start | bytes 18436
  81.9 1.9 copy-start.18
  82.0 14.5 %collective-permute-start.14 = (f32[48,1,130]{2,0,1:T(8,128)S(1)}, f32[48,1,130]{2,0,1:T(8,128)S(1)}, u32[]{:S(2)}, u32[]{:S(2)}) collective-permute-start(f32[48,1,130]{2,0,1:T(8,128)S(1)} %get-tuple-element.249), channel_id=1, source_target_pairs={{0,4},{4,8},{8,12},{12,0},{1,5},{5,9},{9,13},{13,1},{2,6},{6,10},{... | collective-permute-start | bytes 74888 | tf_op jit(solution)/shard_map/ppermute | solution.py:22
  82.2 14.3 %collective-permute-start.15 = (f32[48,1,130]{2,0,1:T(8,128)S(1)}, f32[48,1,130]{2,0,1:T(8,128)S(1)}, u32[]{:S(2)}, u32[]{:S(2)}) collective-permute-start(f32[48,1,130]{2,0,1:T(8,128)S(1)} %get-tuple-element.250), channel_id=1, source_target_pairs={{4,0},{8,4},{12,8},{0,12},{5,1},{9,5},{13,9},{1,13},{6,2},{10,6},{... | collective-permute-start | bytes 74888 | tf_op jit(solution)/shard_map/ppermute | solution.py:25
  83.9 5.6 collective-permute-start.9
  94.2 6.0 copy-start.15
  94.3 12.4 %collective-permute-start.10 = (f32[52,36,6]{0,1,2:T(8,128)S(1)}, f32[52,36,6]{0,1,2:T(8,128)S(1)}, u32[]{:S(2)}, u32[]{:S(2)}) collective-permute-start(f32[52,36,6]{0,1,2:T(8,128)S(1)} %copy.15), channel_id=1, source_target_pairs={{0,16},{16,32},{32,48},{48,64},{64,80},{80,96},{96,112},{112,0},{1... | collective-permute-start | bytes 134792 | tf_op jit(solution)/shard_map/ppermute | solution.py:22
  96.8 49.3 %collective-permute-start.16 = (f32[1,34,130]{2,0,1:T(1,128)S(1)}, f32[1,34,130]{2,0,1:T(1,128)S(1)}, u32[]{:S(2)}, u32[]{:S(2)}) collective-permute-start(f32[1,34,130]{2,0,1:T(1,128)S(1)} %get-tuple-element.243), channel_id=1, source_target_pairs={{0,1},{1,2},{2,3},{3,0},{4,5},{5,6},{6,7},{7,4},{8,9},{9,10},{10,1... | collective-permute-start | bytes 53048 | tf_op jit(solution)/shard_map/ppermute | solution.py:22
  97.2 48.8 %collective-permute-start.17 = (f32[1,34,130]{2,0,1:T(1,128)S(1)}, f32[1,34,130]{2,0,1:T(1,128)S(1)}, u32[]{:S(2)}, u32[]{:S(2)}) collective-permute-start(f32[1,34,130]{2,0,1:T(1,128)S(1)} %get-tuple-element.244), channel_id=1, source_target_pairs={{1,0},{2,1},{3,2},{0,3},{5,4},{6,5},{7,6},{4,7},{9,8},{10,9},{11,1... | collective-permute-start | bytes 53048 | tf_op jit(solution)/shard_map/ppermute | solution.py:25
  102.5 20.9 %collective-permute-start.11 = (f32[52,36,6]{0,1,2:T(8,128)S(1)}, f32[52,36,6]{0,1,2:T(8,128)}, u32[]{:S(2)}, u32[]{:S(2)}) collective-permute-start(f32[52,36,6]{0,1,2:T(8,128)S(1)} %copy.17), channel_id=1, source_target_pairs={{16,0},{32,16},{48,32},{64,48},{80,64},{96,80},{112,96},{0,112},{1... | collective-permute-start | bytes 134792 | tf_op jit(solution)/shard_map/ppermute | solution.py:25
  146.1 6.0 copy-start.13
  221.6 119.8 %copy-start.2 = (f32[48,32,128]{2,0,1:T(8,128)}, f32[48,32,128]{2,0,1:T(8,128)S(1)}, u32[]{:S(2)}) copy-start(f32[48,32,128]{2,0,1:T(8,128)S(1)} %multiply_subtract_fusion.2) | copy-start | bytes 2359300
  224.5 8.0 %collective-permute-start.18 = (f32[48,32,4]{0,1,2:T(8,128)S(1)}, f32[48,32,4]{0,1,2:T(8,128)S(1)}, u32[]{:S(2)}, u32[]{:S(2)}) collective-permute-start(f32[48,32,4]{0,1,2:T(8,128)S(1)} %copy.26), channel_id=1, source_target_pairs={{0,16},{16,32},{32,48},{48,64},{64,80},{80,96},{96,112},{112,0},{1... | collective-permute-start | bytes 73736 | tf_op jit(solution)/shard_map/ppermute | solution.py:22
  228.8 5.8 collective-permute-start.19
  235.9 7.3 copy-start.19
  235.9 7.3 copy-start.21
  237.2 5.9 collective-permute-start.20
  237.3 5.9 collective-permute-start.21
  243.5 8.2 %collective-permute-start.22 = (f32[4,40,136]{2,0,1:T(4,128)S(1)}, f32[4,40,136]{2,0,1:T(4,128)S(1)}, u32[]{:S(2)}, u32[]{:S(2)}) collective-permute-start(f32[4,40,136]{2,0,1:T(4,128)S(1)} %get-tuple-element.239), channel_id=1, source_target_pairs={{0,1},{1,2},{2,3},{3,0},{4,5},{5,6},{6,7},{7,4},{8,9},{9,10},{10,1... | collective-permute-start | bytes 261128 | tf_op jit(solution)/shard_map/ppermute | solution.py:22
  244.3 7.4 collective-permute-start.23
  270.0 11.2 %collective-permute-start.24 = (f32[6,40,136]{2,0,1:T(8,128)S(1)}, f32[6,40,136]{2,0,1:T(8,128)S(1)}, u32[]{:S(2)}, u32[]{:S(2)}) collective-permute-start(f32[6,40,136]{2,0,1:T(8,128)S(1)} %get-tuple-element.260), channel_id=1, source_target_pairs={{0,1},{1,2},{2,3},{3,0},{4,5},{5,6},{6,7},{7,4},{8,9},{9,10},{10,1... | collective-permute-start | bytes 391688 | tf_op jit(solution)/shard_map/ppermute | solution.py:22
  271.7 13.2 %collective-permute-start.25 = (f32[6,40,136]{2,0,1:T(8,128)}, f32[6,40,136]{2,0,1:T(8,128)}, u32[]{:S(2)}, u32[]{:S(2)}) collective-permute-start(f32[6,40,136]{2,0,1:T(8,128)} %get-tuple-element.259), channel_id=1, source_target_pairs={{1,0},{2,1},{3,2},{0,3},{5,4},{6,5},{7,6},{4,7},{9,8},{10,9},{11,1... | collective-permute-start | bytes 391688 | tf_op jit(solution)/shard_map/ppermute | solution.py:25
  291.1 7.6 %collective-permute-start.26 = (f32[52,6,136]{2,0,1:T(8,128)S(1)}, f32[52,6,136]{2,0,1:T(8,128)S(1)}, u32[]{:S(2)}, u32[]{:S(2)}) collective-permute-start(f32[52,6,136]{2,0,1:T(8,128)S(1)} %get-tuple-element.258), channel_id=1, source_target_pairs={{0,4},{4,8},{8,12},{12,0},{1,5},{5,9},{9,13},{13,1},{2,6},{6,10},{... | collective-permute-start | bytes 509192 | tf_op jit(solution)/shard_map/ppermute | solution.py:22
  292.9 6.9 collective-permute-start.27
  304.5 11.3 %collective-permute-start.28 = (f32[52,36,6]{0,1,2:T(8,128)S(1)}, f32[52,36,6]{0,1,2:T(8,128)}, u32[]{:S(2)}, u32[]{:S(2)}) collective-permute-start(f32[52,36,6]{0,1,2:T(8,128)S(1)} %copy.30), channel_id=1, source_target_pairs={{0,16},{16,32},{32,48},{48,64},{64,80},{80,96},{96,112},{112,0},{1... | collective-permute-start | bytes 134792 | tf_op jit(solution)/shard_map/ppermute | solution.py:22
  312.1 15.0 %collective-permute-start.29 = (f32[52,36,6]{0,1,2:T(8,128)S(1)}, f32[52,36,6]{0,1,2:T(8,128)S(1)}, u32[]{:S(2)}, u32[]{:S(2)}) collective-permute-start(f32[52,36,6]{0,1,2:T(8,128)S(1)} %copy.32), channel_id=1, source_target_pairs={{16,0},{32,16},{48,32},{64,48},{80,64},{96,80},{112,96},{0,112},{1... | collective-permute-start | bytes 134792 | tf_op jit(solution)/shard_map/ppermute | solution.py:25
  409.4 2.0 copy-start.4
  409.4 2.0 copy-start.7
  409.4 2.2 copy-start.10
  411.6 4.7 copy-start
  489.0 8.0 %collective-permute-start.30 = (f32[48,32,4]{0,1,2:T(8,128)S(1)}, f32[48,32,4]{0,1,2:T(8,128)S(1)}, u32[]{:S(2)}, u32[]{:S(2)}) collective-permute-start(f32[48,32,4]{0,1,2:T(8,128)S(1)} %copy.34), channel_id=1, source_target_pairs={{0,16},{16,32},{32,48},{48,64},{64,80},{80,96},{96,112},{112,0},{1... | collective-permute-start | bytes 73736 | tf_op jit(solution)/shard_map/ppermute | solution.py:22
  492.2 6.1 collective-permute-start.31
  499.5 8.5 %copy-start.20 = (f32[48,32,4]{2,0,1:T(8,128)S(1)}, f32[48,32,4]{2,0,1:T(8,128)}, u32[]{:S(2)}) copy-start(f32[48,32,4]{2,0,1:T(8,128)} %copy.36) | copy-start | bytes 73732
  499.5 8.5 %copy-start.22 = (f32[48,32,4]{2,0,1:T(8,128)S(1)}, f32[48,32,4]{2,0,1:T(8,128)}, u32[]{:S(2)}) copy-start(f32[48,32,4]{2,0,1:T(8,128)} %copy.37) | copy-start | bytes 73732
  500.9 7.2 collective-permute-start.32
  500.9 7.1 collective-permute-start.33
  508.3 7.5 collective-permute-start.34
  508.4 7.4 collective-permute-start.35
  534.1 10.2 %collective-permute-start.36 = (f32[6,40,136]{2,0,1:T(8,128)S(1)}, f32[6,40,136]{2,0,1:T(8,128)S(1)}, u32[]{:S(2)}, u32[]{:S(2)}) collective-permute-start(f32[6,40,136]{2,0,1:T(8,128)S(1)} %get-tuple-element.256), channel_id=1, source_target_pairs={{0,1},{1,2},{2,3},{3,0},{4,5},{5,6},{6,7},{7,4},{8,9},{9,10},{10,1... | collective-permute-start | bytes 391688 | tf_op jit(solution)/shard_map/ppermute | solution.py:22
  536.1 11.9 %collective-permute-start.37 = (f32[6,40,136]{2,0,1:T(8,128)}, f32[6,40,136]{2,0,1:T(8,128)}, u32[]{:S(2)}, u32[]{:S(2)}) collective-permute-start(f32[6,40,136]{2,0,1:T(8,128)} %get-tuple-element.255), channel_id=1, source_target_pairs={{1,0},{2,1},{3,2},{0,3},{5,4},{6,5},{7,6},{4,7},{9,8},{10,9},{11,1... | collective-permute-start | bytes 391688 | tf_op jit(solution)/shard_map/ppermute | solution.py:25
  554.1 7.8 %collective-permute-start.38 = (f32[52,6,136]{2,0,1:T(8,128)S(1)}, f32[52,6,136]{2,0,1:T(8,128)S(1)}, u32[]{:S(2)}, u32[]{:S(2)}) collective-permute-start(f32[52,6,136]{2,0,1:T(8,128)S(1)} %get-tuple-element.254), channel_id=1, source_target_pairs={{0,4},{4,8},{8,12},{12,0},{1,5},{5,9},{9,13},{13,1},{2,6},{6,10},{... | collective-permute-start | bytes 509192 | tf_op jit(solution)/shard_map/ppermute | solution.py:22
  555.9 7.0 collective-permute-start.39
  567.8 11.2 %collective-permute-start.40 = (f32[52,36,6]{0,1,2:T(8,128)S(1)}, f32[52,36,6]{0,1,2:T(8,128)}, u32[]{:S(2)}, u32[]{:S(2)}) collective-permute-start(f32[52,36,6]{0,1,2:T(8,128)S(1)} %copy.38), channel_id=1, source_target_pairs={{0,16},{16,32},{32,48},{48,64},{64,80},{80,96},{96,112},{112,0},{1... | collective-permute-start | bytes 134792 | tf_op jit(solution)/shard_map/ppermute | solution.py:22
  575.6 15.0 %collective-permute-start.41 = (f32[52,36,6]{0,1,2:T(8,128)S(1)}, f32[52,36,6]{0,1,2:T(8,128)S(1)}, u32[]{:S(2)}, u32[]{:S(2)}) collective-permute-start(f32[52,36,6]{0,1,2:T(8,128)S(1)} %copy.40), channel_id=1, source_target_pairs={{16,0},{32,16},{48,32},{64,48},{80,64},{96,80},{112,96},{0,112},{1... | collective-permute-start | bytes 134792 | tf_op jit(solution)/shard_map/ppermute | solution.py:25
  673.5 2.7 copy-start.5
  673.5 2.7 copy-start.8
  673.5 2.8 copy-start.11
  676.3 4.7 copy-start.1
  748.0 2.8 copy-start.24
  (3 other events, 3.9 us)
where the time goes:
time: 762 us; the launch traced here: 753 us
  blocking collectives  318 us (42%)
  local copies, waits for them, and re-layouts  159 us (21%)
  starting transfers between devices  78.1 us (10%)
  other arithmetic  71.6 us (9%)
  waiting for transfers between devices  67.7 us (9%)
  matrix products  50.4 us (7%)
  between operations  8.36 us (1%)
    psum x3, blocking collectives, residual_dot(): return lax.psum(local_sum, ('gx', 'gy', 'gz'))  192 us
    psum x2, blocking collectives, per_device(): lax.psum(jnp.sum(direction_core * crop(applied, res_margin)), ('gx', 'gy'...  126 us
    scatter-add x12, local copies, waits for them, and re-layouts, place(): owned.at[tuple(first_cut)].add(below_pad).at[tuple(last_cut)].add(above_pad)  84.6 us
    ppermute x21, waiting for transfers between devices, extended_2(): lax.ppermute(lax.slice_in_dim(block, block.shape[dim] - width, None, axis...  62.2 us
    ppermute x21, starting transfers between devices, extended_2(): lax.ppermute(lax.slice_in_dim(block, 0, width, axis=dim), axis, backward)  60.1 us
    add x12, other arithmetic, place(): owned.at[tuple(first_cut)].add(below_pad).at[tuple(last_cut)].add(above_pad)  21.4 us
    dot_general x6, matrix products, transform(): values = jnp.einsum('zyx,xc->zyc', values, column_table, precision=highest)  19 us
    ppermute x21, starting transfers between devices, extended_2(): lax.ppermute(lax.slice_in_dim(block, block.shape[dim] - width, None, axis...  18 us
  transfers between devices with their start and end apart: 42, of which 18 were waited for; matrix products, arithmetic and copies ran while one was open for 15% of the time, Pallas kernels for 0%

commit v1 on v0

v1 whole, which is shorter than its diff:
```python
import jax
import jax.numpy as jnp
from jax import lax
from jax.sharding import PartitionSpec as P

OV = 4
ITERS = 3
AXES = ("gx", "gy", "gz")

mass_term = 1e-05
split_term = 0.5
bend_mean = 0.1
highest = lax.Precision.HIGHEST


def shifted(block, axis, step):
    count = lax.axis_size(axis)
    return lax.ppermute(block, axis, [(i, (i + step) % count) for i in range(count)])


def extended(block, sides, width):
    for axis, dim in sides:
        low = shifted(
            lax.slice_in_dim(block, block.shape[dim] - width, None, axis=dim), axis, 1
        )
        high = shifted(lax.slice_in_dim(block, 0, width, axis=dim), axis, -1)
        block = jnp.concatenate([low, block, high], axis=dim)
    return block


def sine_table(length):
    places = jnp.arange(1, length + 1, dtype=jnp.float32)
    factor = jnp.sqrt(2.0 / (length + 1.0))
    return factor * jnp.sin(jnp.pi * places[:, None] * places[None, :] / (length + 1.0))


def eigen_line(length):
    places = jnp.arange(1, length + 1, dtype=jnp.float32)
    return 2.0 - 2.0 * jnp.cos(jnp.pi * places / (length + 1.0))


def transform(values, tables):
    depth_table, row_table, column_table = tables
    values = jnp.einsum("zyx,xc->zyc", values, column_table, precision=highest)
    values = jnp.einsum("zyx,yb->zbx", values, row_table, precision=highest)
    return jnp.einsum("zyx,za->ayx", values, depth_table, precision=highest)


def local_solve(values):
    depth_len, row_len, column_len = values.shape
    tables = (sine_table(depth_len), sine_table(row_len), sine_table(column_len))
    spectrum = (
        eigen_line(depth_len)[:, None, None]
        + eigen_line(row_len)[None, :, None]
        + eigen_line(column_len)[None, None, :]
    )
    inverse = 1.0 / (mass_term + bend_mean * spectrum * spectrum + split_term * spectrum)
    return transform(transform(values, tables) * inverse, tables)


def crop(values, margin):
    if margin == 0:
        return values
    return values[margin:-margin, margin:-margin, margin:-margin]


def laplace(values):
    centre = values[1:-1, 1:-1, 1:-1]
    beside = values[2:, 1:-1, 1:-1] + values[:-2, 1:-1, 1:-1]
    beside = beside + values[1:-1, 2:, 1:-1] + values[1:-1, :-2, 1:-1]
    beside = beside + values[1:-1, 1:-1, 2:] + values[1:-1, 1:-1, :-2]
    return 6.0 * centre - beside


def operate(values, value_margin, stiffness, stiff_margin):
    out_margin = value_margin - 2
    flux = laplace(values)
    weighted = crop(stiffness, stiff_margin - out_margin - 1) * flux
    return mass_term * crop(values, 2) + laplace(weighted) + split_term * crop(flux, 1)


def fold(wide, margin):
    rim = OV + margin
    for axis, dim in (("gz", 0), ("gy", 1), ("gx", 2)):
        extent = wide.shape[dim]
        low = shifted(lax.slice_in_dim(wide, extent - rim, extent, axis=dim), axis, 1)
        high = shifted(lax.slice_in_dim(wide, 0, rim, axis=dim), axis, -1)
        length = extent - 2 * OV + 2 * margin
        pads = [(0, 0, 0)] * 3
        grow = margin - OV

        def padded(values, before, after):
            pads[dim] = (before, after, 0)
            return lax.pad(values, jnp.float32(0), pads)

        wide = (
            padded(wide, grow, grow)
            + padded(low, 0, length - rim)
            + padded(high, length - rim, 0)
        )
    return wide


def total(values):
    gz, gy, gx = lax.axis_size("gz"), lax.axis_size("gy"), lax.axis_size("gx")
    for axis, count in (("gx", gx), ("gy", gy), ("gz", gz)):
        hop = 1
        while hop < count:
            values = values + lax.ppermute(values, axis, [(i, i ^ hop) for i in range(count)])
            hop *= 2
    return values


def weights(sums):
    b = sums[:ITERS]
    pair = {}
    at = ITERS
    for i in range(ITERS):
        for j in range(i, ITERS):
            pair[i, j] = pair[j, i] = sums[at]
            at += 1
    sigma = [jnp.float32(0)] * ITERS
    delta = None
    current = None
    for turn in range(ITERS):
        zeta = [jnp.float32(1)] + [-s for s in sigma[:turn]]
        following = sum(z * b[i] for i, z in enumerate(zeta))
        for i, z in enumerate(zeta):
            for j in range(turn):
                following = following - z * sigma[j] * pair[i, j]
        if turn == 0:
            delta = zeta
        else:
            ratio = following / current
            delta = [z + ratio * d for z, d in zip(zeta, delta + [jnp.float32(0)])]
        current = following
        bending = sum(
            delta[i] * delta[j] * pair[i, j] for i in range(turn + 1) for j in range(turn + 1)
        )
        step = current / bending
        sigma = [
            s + step * d for s, d in zip(sigma, delta + [jnp.float32(0)] * (ITERS - turn - 1))
        ]
    return sigma


def per_device(rhs_field, stiffness):
    sides = (("gx", 2), ("gy", 1), ("gz", 0))
    wide = extended(rhs_field, sides, OV)
    stiff_wide = extended(stiffness, sides, OV + 1)
    smooth, image = [], []
    for turn in range(ITERS):
        margin = OV + 2 if turn + 1 < ITERS else 2
        values = fold(local_solve(wide), margin)
        wide = operate(values, margin, stiff_wide, OV + 1)
        smooth.append(crop(values, margin))
        image.append(crop(wide, margin - 2))
    dots = [jnp.sum(rhs_field * u) for u in smooth]
    for i in range(ITERS):
        for j in range(i, ITERS):
            dots.append(jnp.sum(smooth[i] * image[j]))
    sums = total(jnp.stack(dots))
    sigma = weights([sums[i] for i in range(len(dots))])
    solution = sum(s * u for s, u in zip(sigma, smooth))
    residual = rhs_field - sum(s * w for s, w in zip(sigma, image))
    return (solution, residual)


def solution(mesh):
    in_specs = (P("gz", "gy", "gx"), P("gz", "gy", "gx"))
    out_specs = (P("gz", "gy", "gx"), P("gz", "gy", "gx"))
    return jax.shard_map(
        per_device, mesh=mesh, in_specs=in_specs, out_specs=out_specs, check_vma=False
    )
```

time: 762 us -> 358 us (0.47)
  blocking collectives: 318 us -> 0 us
  local copies, waits for them, and re-layouts: 159 us -> 52.1 us
  waiting for transfers between devices: 67.7 us -> 116 us
  starting transfers between devices: 78.1 us -> 57 us
  other arithmetic: 71.6 us -> 60.2 us
  between operations: 8.36 us -> 17 us
    psum x5 -> x0, blocking collectives: 318 us -> none  [the longest x3 192 us: residual_dot(): return lax.psum(local_sum, ('gx', 'gy', 'gz'))]
    scatter-add x12 -> x0, local copies, waits for them, and re-layouts: 84.6 us -> none  [place(): owned.at[tuple(first_cut)].add(below_pad).at[tuple(last_cut)].add(above_pad)]
    ppermute x42 -> x37, waiting for transfers between devices: 67.7 us -> 116 us  [the longest x30 94 us: shifted(): lax.ppermute(block, axis, [(i, (i + step) % count) for i in range(count)])]
    slice x32 -> x22, local copies, waits for them, and re-layouts: 47.1 us -> 23.7 us  [the longest x14 15.3 us: fold(): lax.slice_in_dim(wide, extent - rim, extent, axis=dim)]
    ppermute x42 -> x37, starting transfers between devices: 78.1 us -> 57 us  [the longest x30 52.5 us: shifted(): lax.ppermute(block, axis, [(i, (i + step) % count) for i in range(count)])]
    reduce_sum x5 -> x1, other arithmetic: 14.7 us -> 6.68 us  [per_device(): dots.append(jnp.sum(smooth[i] * image[j]))]
    add x15 -> x19, other arithmetic: 28.8 us -> 30 us  [the longest x9 15.9 us: fold(): padded(wide, grow, grow) + padded(low, 0, length - rim)]
  transfers between devices with their start and end apart: 42 -> 37, of which waited for: 18 -> 24; matrix products, arithmetic and copies ran while one was open for 15% -> 10% of each run, Pallas kernels for 0% -> 0%
where the time goes in v1:
time: 358 us; the launch traced here: 353 us
  waiting for transfers between devices  116 us (32%)
  other arithmetic  60.2 us (17%)
  starting transfers between devices  57 us (16%)
  local copies, waits for them, and re-layouts  52.1 us (15%)
  matrix products  50.5 us (14%)
  between operations  17 us (5%)
    ppermute x30, waiting for transfers between devices, shifted(): lax.ppermute(block, axis, [(i, (i + step) % count) for i in range(count)])  94 us
    ppermute x30, starting transfers between devices, shifted(): lax.ppermute(block, axis, [(i, (i + step) % count) for i in range(count)])  52.5 us
    ppermute x7, waiting for transfers between devices, total(): lax.ppermute(values, axis, [(i, i ^ hop) for i in range(count)])  22.4 us
    dot_general x6, matrix products, transform(): return jnp.einsum('zyx,za->ayx', values, depth_table, precision=highest)  18.7 us
    dot_general x6, matrix products, transform(): values = jnp.einsum('zyx,xc->zyc', values, column_table, precision=highest)  17.9 us
    mul x3, other arithmetic, operate(): weighted = crop(stiffness, stiff_margin - out_margin - 1) * flux  17.5 us
    add x9, other arithmetic, fold(): padded(wide, grow, grow) + padded(low, 0, length - rim)  15.9 us
    slice x14, local copies, waits for them, and re-layouts, fold(): lax.slice_in_dim(wide, extent - rim, extent, axis=dim)  15.3 us
  transfers between devices with their start and end apart: 37, of which 24 were waited for; matrix products, arithmetic and copies ran while one was open for 10% of the time, Pallas kernels for 0%

profile of v1, /device:TPU:0, one launch (start us, length us, event | category | flops | bytes accessed | tf_op | source)
XLA Modules:
  0.0 353.1 jit_solution(103713288834590107)
XLA Ops:
  2.9 6.2 %collective-permute-start.1 = (f32[48,32,4]{0,1,2:T(8,128)S(1)}, f32[48,32,4]{0,1,2:T(8,128)S(1)}, u32[]{:S(2)}, u32[]{:S(2)}) collective-permute-start(f32[48,32,4]{0,1,2:T(8,128)S(1)} %copy.60), channel_id=1, source_target_pairs={{0,112},{16,0},{32,16},{48,32},{64,48},{80,64},{96,80},{112,96},{1... | collective-permute-start | bytes 73736 | tf_op jit(solution)/shard_map/ppermute | solution.py:18
  9.9 7.6 %collective-permute-done = f32[48,32,4]{0,1,2:T(8,128)S(1)} collective-permute-done((f32[48,32,4]{0,1,2:T(8,128)S(1)}, f32[48,32,4]{0,1,2:T(8,128)S(1)}, u32[]{:S(2)}, u32[]{:S(2)}) %collective-permute-start) | collective-permute-done | bytes 24608 | tf_op jit(solution)/shard_map/ppermute | solution.py:18
  21.2 4.1 %collective-permute-done.2 = f32[48,4,136]{2,1,0:T(4,128)S(1)} collective-permute-done((f32[48,4,136]{2,1,0:T(4,128)S(1)}, f32[48,4,136]{2,1,0:T(4,128)S(1)}, u32[]{:S(2)}, u32[]{:S(2)}) %collective-permute-start.2) | collective-permute-done | bytes 104480 | tf_op jit(solution)/shard_map/ppermute | solution.py:18
  29.3 4.3 %collective-permute-done.4 = f32[4,40,136]{2,1,0:T(8,128)S(1)} collective-permute-done((f32[4,40,136]{2,1,0:T(8,128)S(1)}, f32[4,40,136]{2,1,0:T(8,128)S(1)}, u32[]{:S(2)}, u32[]{:S(2)}) %collective-permute-start.4) | collective-permute-done | bytes 87072 | tf_op jit(solution)/shard_map/ppermute | solution.py:18
  34.6 3.1 fusion.12
  37.7 2.2 fusion.115
  39.9 3.3 fusion.57
  43.2 3.0 fusion.51
  46.2 2.4 fusion.113
  48.6 2.9 fusion.34
  51.8 2.9 collective-permute-start.7
  55.1 8.7 %collective-permute-done.7 = f32[10,40,136]{2,1,0:T(8,128)S(1)} collective-permute-done((f32[10,40,136]{2,1,0:T(8,128)S(1)}, f32[10,40,136]{2,1,0:T(8,128)S(1)}, u32[]{:S(2)}, u32[]{:S(2)}) %collective-permute-start.7) | collective-permute-done | bytes 217632 | tf_op jit(solution)/shard_map/ppermute | solution.py:18
  63.9 3.6 %collective-permute-done.6 = f32[10,40,136]{2,1,0:T(8,128)S(1)} collective-permute-done((f32[10,40,136]{2,1,0:T(8,128)S(1)}, f32[10,40,136]{2,1,0:T(8,128)S(1)}, u32[]{:S(2)}, u32[]{:S(2)}) %collective-permute-start.6) | collective-permute-done | bytes 217632 | tf_op jit(solution)/shard_map/ppermute | solution.py:18
  75.7 5.7 %collective-permute-start.13 = (f32[48,32,5]{0,1,2:T(8,128)S(1)}, f32[48,32,5]{0,1,2:T(8,128)S(1)}, u32[]{:S(2)}, u32[]{:S(2)}) collective-permute-start(f32[48,32,5]{0,1,2:T(8,128)S(1)} %copy.62), channel_id=1, source_target_pairs={{0,112},{16,0},{32,16},{48,32},{64,48},{80,64},{96,80},{112,96},{1... | collective-permute-start | bytes 92168 | tf_op jit(solution)/shard_map/ppermute | solution.py:18
  83.0 5.7 %collective-permute-done.12 = f32[48,32,5]{0,1,2:T(8,128)S(1)} collective-permute-done((f32[48,32,5]{0,1,2:T(8,128)S(1)}, f32[48,32,5]{0,1,2:T(8,128)S(1)}, u32[]{:S(2)}, u32[]{:S(2)}) %collective-permute-start.12) | collective-permute-done | bytes 30752 | tf_op jit(solution)/shard_map/ppermute | solution.py:18
  92.2 2.6 pad_add_fusion.3
  94.8 2.5 fusion.210
  97.3 2.8 copy.21
  102.1 3.3 collective-permute-start.11
  107.6 3.2 collective-permute-start.17
  110.8 6.5 %collective-permute-done.10 = f32[60,44,10]{0,1,2:T(8,128)} collective-permute-done((f32[60,44,10]{0,1,2:T(8,128)}, f32[60,44,10]{0,1,2:T(8,128)}, u32[]{:S(2)}, u32[]{:S(2)}) %collective-permute-start.10) | collective-permute-done | bytes 105632 | tf_op jit(solution)/shard_map/ppermute | solution.py:18
  117.3 2.6 copy.22
  121.7 4.0 %pad_add_fusion.2 = f32[60,44,140]{2,0,1:T(8,128)S(1)} fusion(f32[60,44,10]{2,0,1:T(8,128)} %copy.24, f32[60,44,10]{2,0,1:T(8,128)} %copy.22, f32[60,44,136]{2,0,1:T(8,128)} %copy-done.5), kind=kLoop, calls=%fused_computation.5 | loop fusion | flops 739200 | bytes 3125760 | tf_op jit(solution)/shard_map/add | solution.py:97
  125.8 9.3 %fusion.207 = (f32[58,42,138]{2,0,1:T(8,128)S(1)}, f32[58,42,138]{2,0,1:T(8,128)}, f32[58,42,138]{2,0,1:T(8,128)S(1)}) fusion(f32[5,42,138]{2,0,1:T(8,128)} %collective-permute-done.17, f32[48,5,138]{2,0,1:T(8,128)S(1)} %collective-permute-done.15, f32[48,32,5]{2,0,1:T(8,128)S(1)} %copy-done.21, f32[48,32,128]{2,0,1:T(8,128)S(1)} %copy-done.15, ...), kind=kLoop, calls=%fused_computation.292 | loop fusion | flops 4706352 | bytes 14791392 | tf_op jit(solution)/shard_map/mul | solution.py:78
  135.1 5.8 %fusion.9 = f32[56,40,136]{2,0,1:T(8,128)S(1)} fusion(f32[58,42,138]{2,0,1:T(8,128)S(1)} %get-tuple-element.32, f32[58,42,138]{2,0,1:T(8,128)S(1)} %get-tuple-element.30, f32[60,44,140]{2,0,1:T(8,128)S(1)} %pad_add_fusion.2), kind=kLoop, calls=%fused_computation.41 | loop fusion | flops 3351040 | bytes 12185600 | tf_op jit(solution)/shard_map/add | solution.py:79
  140.9 2.9 fusion.48
  143.8 2.2 fusion.111
  146.0 3.4 fusion.60
  149.4 2.9 fusion.45
  152.3 2.4 fusion.109
  154.7 2.9 fusion.30
  160.4 8.4 %collective-permute-done.19 = f32[10,40,136]{2,1,0:T(8,128)S(1)} collective-permute-done((f32[10,40,136]{2,1,0:T(8,128)S(1)}, f32[10,40,136]{2,1,0:T(8,128)S(1)}, u32[]{:S(2)}, u32[]{:S(2)}) %collective-permute-start.19) | collective-permute-done | bytes 217632 | tf_op jit(solution)/shard_map/ppermute | solution.py:18
  172.9 15.2 %collective-permute-done.20 = f32[60,10,136]{2,0,1:T(8,128)S(1)} collective-permute-done((f32[60,10,136]{2,0,1:T(8,128)S(1)}, f32[60,10,136]{2,0,1:T(8,128)S(1)}, u32[]{:S(2)}, u32[]{:S(2)}) %collective-permute-start.20) | collective-permute-done | bytes 326432 | tf_op jit(solution)/shard_map/ppermute | solution.py:18
  188.6 2.5 fusion.209
  193.2 3.5 collective-permute-start.22
  197.2 2.3 collective-permute-start.23
  199.5 8.2 %collective-permute-done.22 = f32[60,44,10]{0,1,2:T(8,128)S(1)} collective-permute-done((f32[60,44,10]{0,1,2:T(8,128)S(1)}, f32[60,44,10]{0,1,2:T(8,128)S(1)}, u32[]{:S(2)}, u32[]{:S(2)}) %collective-permute-start.22) | collective-permute-done | bytes 105632 | tf_op jit(solution)/shard_map/ppermute | solution.py:18
  211.8 4.0 %pad_add_fusion = f32[60,44,140]{2,0,1:T(8,128)S(1)} fusion(f32[60,44,10]{2,0,1:T(8,128)} %copy.38, f32[60,44,10]{2,0,1:T(8,128)} %copy.36, f32[60,44,136]{2,0,1:T(8,128)} %copy-done.6), kind=kLoop, calls=%fused_computation.3 | loop fusion | flops 739200 | bytes 3125760 | tf_op jit(solution)/shard_map/add | solution.py:97
  215.8 4.6 %fusion.205 = (f32[58,42,138]{2,0,1:T(8,128)S(1)}, f32[58,42,138]{2,0,1:T(8,128)S(1)}) fusion(f32[58,42,138]{2,0,1:T(8,128)S(1)} %copy-done.7, f32[60,44,140]{2,0,1:T(8,128)S(1)} %pad_add_fusion), kind=kLoop, calls=%fused_computation.291 | loop fusion | flops 2689344 | bytes 13446720 | tf_op jit(solution)/shard_map/mul | solution.py:78
  220.4 5.5 %fusion.6 = f32[56,40,136]{2,0,1:T(8,128)S(1)} fusion(f32[58,42,138]{2,0,1:T(8,128)S(1)} %get-tuple-element.29, f32[58,42,138]{2,0,1:T(8,128)S(1)} %get-tuple-element.28, f32[60,44,140]{2,0,1:T(8,128)S(1)} %pad_add_fusion), kind=kLoop, calls=%fused_computation.30 | loop fusion | flops 3351040 | bytes 12185600 | tf_op jit(solution)/shard_map/add | solution.py:79
  225.9 3.0 fusion.42
  228.9 2.2 fusion.107
  231.1 3.4 fusion.63
  234.5 3.0 fusion.39
  237.5 2.6 fusion.105
  240.1 2.9 fusion.26
  243.7 2.7 collective-permute-start.25
  246.4 7.6 %collective-permute-done.24 = f32[6,40,136]{2,0,1:T(8,128)S(1)} collective-permute-done((f32[6,40,136]{2,0,1:T(8,128)S(1)}, f32[6,40,136]{2,0,1:T(8,128)S(1)}, u32[]{:S(2)}, u32[]{:S(2)}) %collective-permute-start.24) | collective-permute-done | bytes 130592 | tf_op jit(solution)/shard_map/ppermute | solution.py:18
  256.2 8.5 %collective-permute-done.26 = f32[52,6,136]{2,0,1:T(8,128)S(1)} collective-permute-done((f32[52,6,136]{2,0,1:T(8,128)S(1)}, f32[52,6,136]{2,0,1:T(8,128)S(1)}, u32[]{:S(2)}, u32[]{:S(2)}) %collective-permute-start.26) | collective-permute-done | bytes 169760 | tf_op jit(solution)/shard_map/ppermute | solution.py:18
  269.5 2.4 collective-permute-start.28
  273.5 3.6 %collective-permute-start.29 = (f32[52,36,6]{0,1,2:T(8,128)S(1)}, f32[52,36,6]{0,1,2:T(8,128)S(1)}, u32[]{:S(2)}, u32[]{:S(2)}) collective-permute-start(f32[52,36,6]{0,1,2:T(8,128)S(1)} %copy.42), channel_id=1, source_target_pairs={{0,112},{16,0},{32,16},{48,32},{64,48},{80,64},{96,80},{112,96},{1... | collective-permute-start | bytes 134792 | tf_op jit(solution)/shard_map/ppermute | solution.py:18
  282.4 3.4 fusion.54
  285.9 3.7 %slice_multiply_fusion.9 = (f32[50,34,130]{2,0,1:T(8,128)S(1)}, f32[50,34,130]{2,0,1:T(8,128)S(1)}) fusion(f32[58,42,138]{2,0,1:T(8,128)S(1)} %copy-done.8, f32[52,36,132]{2,0,1:T(8,128)S(1)} %fusion.54), kind=kLoop, calls=%fused_computation.104 | loop fusion | flops 1768000 | bytes 8840000 | tf_op jit(solution)/shard_map/mul | solution.py:78
  289.5 6.7 %multiply_reduce_fusion = (f32[]{:T(128)}, f32[]{:T(128)}, f32[]{:T(128)}, f32[]{:T(128)}, f32[]{:T(128)}, /*index=5*/f32[]{:T(128)}, f32[]{:T(128)}, f32[]{:T(128)}, f32[]{:T(128)}, f32[48,32,128]{2,0,1:T(8,128)}) fusion(f32[52,36,132]{2,0,1:T(8,128)S(1)} %fusion.54, f32[48,32,128]{2,1,0:T(8,128)S(1)} %copy-done.3, f32[60,44,140]{2,0,1:T(8,128)} %copy-done, ...), kind=kLoop, calls=%fused_computation.120 | loop fusion | flops 5701623 | bytes 11796516 | tf_op jit(solution)/shard_map/reduce_sum | solution.py:161
  296.2 5.6 %stack.39 = f32[9]{0:T(128)S(1)} concatenate(f32[1]{0:T(128)} %bitcast.5, f32[1]{0:T(128)} %bitcast.8, f32[1]{0:T(128)} %bitcast.11, f32[1]{0:T(128)} %bitcast.12, f32[1]{0:T(128)} %bitcast.13, f32[1]{0:T(128)} %bitcast.14, f32[1]{0:T(128)} %bitcast.15, f32[1]{0:T(128)} %bitcast.16, f32[1]{0:T(128)} %bitcast.17), dimensions={0} | concatenate | bytes 72 | tf_op jit(solution)/shard_map/stack | solution.py:162
  302.9 4.0 %collective-permute-done.30 = f32[9]{0:T(128)S(1)} collective-permute-done((f32[9]{0:T(128)S(1)}, f32[9]{0:T(128)S(1)}, u32[]{:S(2)}, u32[]{:S(2)}) %collective-permute-start.30) | collective-permute-done | bytes 68 | tf_op jit(solution)/shard_map/ppermute | solution.py:109
  306.9 3.5 %collective-permute-done.31 = f32[9]{0:T(128)S(1)} collective-permute-done((f32[9]{0:T(128)S(1)}, f32[9]{0:T(128)S(1)}, u32[]{:S(2)}, u32[]{:S(2)}) %collective-permute-start.31) | collective-permute-done | bytes 68 | tf_op jit(solution)/shard_map/ppermute | solution.py:109
  311.5 3.9 %collective-permute-done.32 = f32[9]{0:T(128)S(1)} collective-permute-done((f32[9]{0:T(128)S(1)}, f32[9]{0:T(128)S(1)}, u32[]{:S(2)}, u32[]{:S(2)}) %collective-permute-start.32) | collective-permute-done | bytes 68 | tf_op jit(solution)/shard_map/ppermute | solution.py:109
  316.6 3.5 %collective-permute-done.34 = f32[9]{0:T(128)S(1)} collective-permute-done((f32[9]{0:T(128)S(1)}, f32[9]{0:T(128)S(1)}, u32[]{:S(2)}, u32[]{:S(2)}) %collective-permute-start.34) | collective-permute-done | bytes 68 | tf_op jit(solution)/shard_map/ppermute | solution.py:109
  320.2 3.5 %collective-permute-done.35 = f32[9]{0:T(128)S(1)} collective-permute-done((f32[9]{0:T(128)S(1)}, f32[9]{0:T(128)S(1)}, u32[]{:S(2)}, u32[]{:S(2)}) %collective-permute-start.35) | collective-permute-done | bytes 68 | tf_op jit(solution)/shard_map/ppermute | solution.py:109
  323.7 2.4 collective-permute-start.36
  326.1 2.7 collective-permute-done.36
  344.9 2.9 multiply_add_fusion
  347.7 2.9 add_subtract_fusion
  (157 shorter events, 66.4 us)
Async XLA Ops:
  2.4 16.6 %copy-start.2 = (f32[48,32,128]{2,1,0:T(8,128)S(1)}, f32[48,32,128]{2,1,0:T(8,128)}, u32[]{:S(2)}) copy-start(f32[48,32,128]{2,1,0:T(8,128)} %param.2) | copy-start | bytes 2359300
  2.9 15.4 %collective-permute-start.1 = (f32[48,32,4]{0,1,2:T(8,128)S(1)}, f32[48,32,4]{0,1,2:T(8,128)S(1)}, u32[]{:S(2)}, u32[]{:S(2)}) collective-permute-start(f32[48,32,4]{0,1,2:T(8,128)S(1)} %copy.60), channel_id=1, source_target_pairs={{0,112},{16,0},{32,16},{48,32},{64,48},{80,64},{96,80},{112,96},{1... | collective-permute-start | bytes 73736 | tf_op jit(solution)/shard_map/ppermute | solution.py:18
  9.5 7.9 %collective-permute-start = (f32[48,32,4]{0,1,2:T(8,128)S(1)}, f32[48,32,4]{0,1,2:T(8,128)S(1)}, u32[]{:S(2)}, u32[]{:S(2)}) collective-permute-start(f32[48,32,4]{0,1,2:T(8,128)S(1)} %copy.59), channel_id=1, source_target_pairs={{0,16},{16,32},{32,48},{48,64},{64,80},{80,96},{96,112},{112,0},{1... | collective-permute-start | bytes 73736 | tf_op jit(solution)/shard_map/ppermute | solution.py:18
  19.4 5.9 %collective-permute-start.2 = (f32[48,4,136]{2,1,0:T(4,128)S(1)}, f32[48,4,136]{2,1,0:T(4,128)S(1)}, u32[]{:S(2)}, u32[]{:S(2)}) collective-permute-start(f32[48,4,136]{2,1,0:T(4,128)S(1)} %get-tuple-element.45), channel_id=1, source_target_pairs={{0,4},{4,8},{8,12},{12,0},{1,5},{5,9},{9,13},{13,1},{2,6},{6,10},{... | collective-permute-start | bytes 313352 | tf_op jit(solution)/shard_map/ppermute | solution.py:18
  19.5 5.8 %collective-permute-start.3 = (f32[48,4,136]{2,1,0:T(4,128)S(1)}, f32[48,4,136]{2,1,0:T(4,128)S(1)}, u32[]{:S(2)}, u32[]{:S(2)}) collective-permute-start(f32[48,4,136]{2,1,0:T(4,128)S(1)} %get-tuple-element.46), channel_id=1, source_target_pairs={{0,12},{4,0},{8,4},{12,8},{1,13},{5,1},{9,5},{13,9},{2,14},{6,2},{... | collective-permute-start | bytes 313352 | tf_op jit(solution)/shard_map/ppermute | solution.py:18
  25.5 8.1 %collective-permute-start.4 = (f32[4,40,136]{2,1,0:T(8,128)S(1)}, f32[4,40,136]{2,1,0:T(8,128)S(1)}, u32[]{:S(2)}, u32[]{:S(2)}) collective-permute-start(f32[4,40,136]{2,1,0:T(8,128)S(1)} %get-tuple-element.39), channel_id=1, source_target_pairs={{0,1},{1,2},{2,3},{3,0},{4,5},{5,6},{6,7},{7,4},{8,9},{9,10},{10,1... | collective-permute-start | bytes 261128 | tf_op jit(solution)/shard_map/ppermute | solution.py:18
  27.1 7.4 %collective-permute-start.5 = (f32[4,40,136]{2,1,0:T(8,128)S(1)}, f32[4,40,136]{2,1,0:T(8,128)S(1)}, u32[]{:S(2)}, u32[]{:S(2)}) collective-permute-start(f32[4,40,136]{2,1,0:T(8,128)S(1)} %get-tuple-element.40), channel_id=1, source_target_pairs={{0,3},{1,0},{2,1},{3,2},{4,7},{5,4},{6,5},{7,6},{8,11},{9,8},{10,9... | collective-permute-start | bytes 261128 | tf_op jit(solution)/shard_map/ppermute | solution.py:18
  51.8 11.9 %collective-permute-start.7 = (f32[10,40,136]{2,1,0:T(8,128)S(1)}, f32[10,40,136]{2,1,0:T(8,128)S(1)}, u32[]{:S(2)}, u32[]{:S(2)}) collective-permute-start(f32[10,40,136]{2,1,0:T(8,128)S(1)} %copy.19), channel_id=1, source_target_pairs={{0,3},{1,0},{2,1},{3,2},{4,7},{5,4},{6,5},{7,6},{8,11},{9,8},{10,9... | collective-permute-start | bytes 652808 | tf_op jit(solution)/shard_map/ppermute | solution.py:18
  55.0 12.5 %collective-permute-start.6 = (f32[10,40,136]{2,1,0:T(8,128)S(1)}, f32[10,40,136]{2,1,0:T(8,128)S(1)}, u32[]{:S(2)}, u32[]{:S(2)}) collective-permute-start(f32[10,40,136]{2,1,0:T(8,128)S(1)} %copy.17), channel_id=1, source_target_pairs={{0,1},{1,2},{2,3},{3,0},{4,5},{5,6},{6,7},{7,4},{8,9},{9,10},{10,1... | collective-permute-start | bytes 652808 | tf_op jit(solution)/shard_map/ppermute | solution.py:18
  68.1 4.4 %copy-start.12 = (f32[60,40,136]{2,0,1:T(8,128)}, f32[60,40,136]{2,0,1:T(8,128)S(1)}, u32[]{:S(2)}) copy-start(f32[60,40,136]{2,0,1:T(8,128)S(1)} %pad_add_fusion.5) | copy-start | bytes 3916804
  68.1 2.9 copy-start.22
  69.3 22.9 %collective-permute-start.8 = (f32[60,10,136]{2,0,1:T(8,128)}, f32[60,10,136]{2,0,1:T(8,128)}, u32[]{:S(2)}, u32[]{:S(2)}) collective-permute-start(f32[60,10,136]{2,0,1:T(8,128)} %get-tuple-element.43), channel_id=1, source_target_pairs={{0,4},{4,8},{8,12},{12,0},{1,5},{5,9},{9,13},{13,1},{2,6},{6,10},{... | collective-permute-start | bytes 979208 | tf_op jit(solution)/shard_map/ppermute | solution.py:18
  69.3 22.9 %collective-permute-start.9 = (f32[60,10,136]{2,0,1:T(8,128)}, f32[60,10,136]{2,0,1:T(8,128)}, u32[]{:S(2)}, u32[]{:S(2)}) collective-permute-start(f32[60,10,136]{2,0,1:T(8,128)} %get-tuple-element.44), channel_id=1, source_target_pairs={{0,12},{4,0},{8,4},{12,8},{1,13},{5,1},{9,5},{13,9},{2,14},{6,2},{... | collective-permute-start | bytes 979208 | tf_op jit(solution)/shard_map/ppermute | solution.py:18
  74.0 14.6 %collective-permute-start.12 = (f32[48,32,5]{0,1,2:T(8,128)S(1)}, f32[48,32,5]{0,1,2:T(8,128)S(1)}, u32[]{:S(2)}, u32[]{:S(2)}) collective-permute-start(f32[48,32,5]{0,1,2:T(8,128)S(1)} %copy.61), channel_id=1, source_target_pairs={{0,16},{16,32},{32,48},{48,64},{64,80},{80,96},{96,112},{112,0},{1... | collective-permute-start | bytes 92168 | tf_op jit(solution)/shard_map/ppermute | solution.py:18
  75.7 13.3 %collective-permute-start.13 = (f32[48,32,5]{0,1,2:T(8,128)S(1)}, f32[48,32,5]{0,1,2:T(8,128)S(1)}, u32[]{:S(2)}, u32[]{:S(2)}) collective-permute-start(f32[48,32,5]{0,1,2:T(8,128)S(1)} %copy.62), channel_id=1, source_target_pairs={{0,112},{16,0},{32,16},{48,32},{64,48},{80,64},{96,80},{112,96},{1... | collective-permute-start | bytes 92168 | tf_op jit(solution)/shard_map/ppermute | solution.py:18
  83.0 7.5 %copy-start.13 = (f32[48,32,128]{2,0,1:T(8,128)}, f32[48,32,128]{2,0,1:T(8,128)S(1)}, u32[]{:S(2)}) copy-start(f32[48,32,128]{2,0,1:T(8,128)S(1)} %copy.29) | copy-start | bytes 2359300
  89.0 3.2 copy-start.16
  89.3 2.8 copy-start.19
  90.4 16.0 %collective-permute-start.14 = (f32[48,5,138]{2,0,1:T(8,128)}, f32[48,5,138]{2,0,1:T(8,128)S(1)}, u32[]{:S(2)}, u32[]{:S(2)}) collective-permute-start(f32[48,5,138]{2,0,1:T(8,128)} %get-tuple-element.47), channel_id=1, source_target_pairs={{0,4},{4,8},{8,12},{12,0},{1,5},{5,9},{9,13},{13,1},{2,6},{6,10},{... | collective-permute-start | bytes 397448 | tf_op jit(solution)/shard_map/ppermute | solution.py:18
  90.4 16.0 %collective-permute-start.15 = (f32[48,5,138]{2,0,1:T(8,128)}, f32[48,5,138]{2,0,1:T(8,128)S(1)}, u32[]{:S(2)}, u32[]{:S(2)}) collective-permute-start(f32[48,5,138]{2,0,1:T(8,128)} %get-tuple-element.48), channel_id=1, source_target_pairs={{0,12},{4,0},{8,4},{12,8},{1,13},{5,1},{9,5},{13,9},{2,14},{6,2},{... | collective-permute-start | bytes 397448 | tf_op jit(solution)/shard_map/ppermute | solution.py:18
  94.8 2.5 copy-start.5
  97.3 9.1 %copy-start.14 = (f32[48,32,128]{2,0,1:T(8,128)S(1)}, f32[48,32,128]{2,0,1:T(8,128)}, u32[]{:S(2)}) copy-start(f32[48,32,128]{2,0,1:T(8,128)} %copy-done.13) | copy-start | bytes 2359300
  97.3 9.1 %copy-start.17 = (f32[48,32,5]{2,0,1:T(8,128)S(1)}, f32[48,32,5]{2,0,1:T(8,128)}, u32[]{:S(2)}) copy-start(f32[48,32,5]{2,0,1:T(8,128)} %copy-done.16) | copy-start | bytes 92164
  97.3 9.1 %copy-start.20 = (f32[48,32,5]{2,0,1:T(8,128)S(1)}, f32[48,32,5]{2,0,1:T(8,128)}, u32[]{:S(2)}) copy-start(f32[48,32,5]{2,0,1:T(8,128)} %copy-done.19) | copy-start | bytes 92164
  102.1 17.9 %collective-permute-start.11 = (f32[60,44,10]{0,1,2:T(8,128)S(1)}, f32[60,44,10]{0,1,2:T(8,128)S(1)}, u32[]{:S(2)}, u32[]{:S(2)}) collective-permute-start(f32[60,44,10]{0,1,2:T(8,128)S(1)} %copy.23), channel_id=1, source_target_pairs={{0,112},{16,0},{32,16},{48,32},{64,48},{80,64},{96,80},{112,96},{1... | collective-permute-start | bytes 316808 | tf_op jit(solution)/shard_map/ppermute | solution.py:18
  105.4 11.9 %collective-permute-start.10 = (f32[60,44,10]{0,1,2:T(8,128)}, f32[60,44,10]{0,1,2:T(8,128)}, u32[]{:S(2)}, u32[]{:S(2)}) collective-permute-start(f32[60,44,10]{0,1,2:T(8,128)} %copy.21), channel_id=1, source_target_pairs={{0,16},{16,32},{32,48},{48,64},{64,80},{80,96},{96,112},{112,0},{1... | collective-permute-start | bytes 316808 | tf_op jit(solution)/shard_map/ppermute | solution.py:18
  107.6 18.1 %collective-permute-start.16 = (f32[5,42,138]{2,0,1:T(8,128)}, f32[5,42,138]{2,0,1:T(8,128)}, u32[]{:S(2)}, u32[]{:S(2)}) collective-permute-start(f32[5,42,138]{2,0,1:T(8,128)} %get-tuple-element.37), channel_id=1, source_target_pairs={{0,1},{1,2},{2,3},{3,0},{4,5},{5,6},{6,7},{7,4},{8,9},{9,10},{10,1... | collective-permute-start | bytes 347768 | tf_op jit(solution)/shard_map/ppermute | solution.py:18
  107.6 18.1 %collective-permute-start.17 = (f32[5,42,138]{2,0,1:T(8,128)}, f32[5,42,138]{2,0,1:T(8,128)}, u32[]{:S(2)}, u32[]{:S(2)}) collective-permute-start(f32[5,42,138]{2,0,1:T(8,128)} %get-tuple-element.38), channel_id=1, source_target_pairs={{0,3},{1,0},{2,1},{3,2},{4,7},{5,4},{6,5},{7,6},{8,11},{9,8},{10,9... | collective-permute-start | bytes 347768 | tf_op jit(solution)/shard_map/ppermute | solution.py:18
  121.7 4.1 %copy-start.15 = (f32[48,32,128]{2,0,1:T(8,128)S(1)}, f32[48,32,128]{2,0,1:T(8,128)}, u32[]{:S(2)}) copy-start(f32[48,32,128]{2,0,1:T(8,128)} %copy-done.13) | copy-start | bytes 2359300
  121.7 4.1 %copy-start.18 = (f32[48,32,5]{2,0,1:T(8,128)S(1)}, f32[48,32,5]{2,0,1:T(8,128)}, u32[]{:S(2)}) copy-start(f32[48,32,5]{2,0,1:T(8,128)} %copy-done.16) | copy-start | bytes 92164
  121.7 4.1 %copy-start.21 = (f32[48,32,5]{2,0,1:T(8,128)S(1)}, f32[48,32,5]{2,0,1:T(8,128)}, u32[]{:S(2)}) copy-start(f32[48,32,5]{2,0,1:T(8,128)} %copy-done.19) | copy-start | bytes 92164
  125.7 9.4 %copy-start = (f32[60,44,140]{2,0,1:T(8,128)}, f32[60,44,140]{2,0,1:T(8,128)S(1)}, u32[]{:S(2)}) copy-start(f32[60,44,140]{2,0,1:T(8,128)S(1)} %pad_add_fusion.2) | copy-start | bytes 4435204
  140.9 2.9 copy-start.10
  158.0 10.8 %collective-permute-start.19 = (f32[10,40,136]{2,1,0:T(8,128)S(1)}, f32[10,40,136]{2,1,0:T(8,128)S(1)}, u32[]{:S(2)}, u32[]{:S(2)}) collective-permute-start(f32[10,40,136]{2,1,0:T(8,128)S(1)} %copy.33), channel_id=1, source_target_pairs={{0,3},{1,0},{2,1},{3,2},{4,7},{5,4},{6,5},{7,6},{8,11},{9,8},{10,9... | collective-permute-start | bytes 652808 | tf_op jit(solution)/shard_map/ppermute | solution.py:18
  158.4 11.9 %collective-permute-start.18 = (f32[10,40,136]{2,1,0:T(8,128)S(1)}, f32[10,40,136]{2,1,0:T(8,128)S(1)}, u32[]{:S(2)}, u32[]{:S(2)}) collective-permute-start(f32[10,40,136]{2,1,0:T(8,128)S(1)} %copy.31), channel_id=1, source_target_pairs={{0,1},{1,2},{2,3},{3,0},{4,5},{5,6},{6,7},{7,4},{8,9},{9,10},{10,1... | collective-permute-start | bytes 652808 | tf_op jit(solution)/shard_map/ppermute | solution.py:18
  171.1 17.0 %collective-permute-start.20 = (f32[60,10,136]{2,0,1:T(8,128)S(1)}, f32[60,10,136]{2,0,1:T(8,128)S(1)}, u32[]{:S(2)}, u32[]{:S(2)}) collective-permute-start(f32[60,10,136]{2,0,1:T(8,128)S(1)} %get-tuple-element.41), channel_id=1, source_target_pairs={{0,4},{4,8},{8,12},{12,0},{1,5},{5,9},{9,13},{13,1},{2,6},{6,10},{... | collective-permute-start | bytes 979208 | tf_op jit(solution)/shard_map/ppermute | solution.py:18
  171.2 17.0 %collective-permute-start.21 = (f32[60,10,136]{2,0,1:T(8,128)S(1)}, f32[60,10,136]{2,0,1:T(8,128)S(1)}, u32[]{:S(2)}, u32[]{:S(2)}) collective-permute-start(f32[60,10,136]{2,0,1:T(8,128)S(1)} %get-tuple-element.42), channel_id=1, source_target_pairs={{0,12},{4,0},{8,4},{12,8},{1,13},{5,1},{9,5},{13,9},{2,14},{6,2},{... | collective-permute-start | bytes 979208 | tf_op jit(solution)/shard_map/ppermute | solution.py:18
  188.6 2.5 copy-start.6
  191.1 5.5 %copy-start.23 = (f32[60,44,10]{2,0,1:T(8,128)S(1)}, f32[60,44,10]{2,0,1:T(8,128)}, u32[]{:S(2)}) copy-start(f32[60,44,10]{2,0,1:T(8,128)} %get-tuple-element.34) | copy-start | bytes 316804
  193.2 14.6 %collective-permute-start.22 = (f32[60,44,10]{0,1,2:T(8,128)S(1)}, f32[60,44,10]{0,1,2:T(8,128)S(1)}, u32[]{:S(2)}, u32[]{:S(2)}) collective-permute-start(f32[60,44,10]{0,1,2:T(8,128)S(1)} %copy.35), channel_id=1, source_target_pairs={{0,16},{16,32},{32,48},{48,64},{64,80},{80,96},{96,112},{112,0},{1... | collective-permute-start | bytes 316808 | tf_op jit(solution)/shard_map/ppermute | solution.py:18
  197.2 12.9 %collective-permute-start.23 = (f32[60,44,10]{0,1,2:T(8,128)S(1)}, f32[60,44,10]{0,1,2:T(8,128)S(1)}, u32[]{:S(2)}, u32[]{:S(2)}) collective-permute-start(f32[60,44,10]{0,1,2:T(8,128)S(1)} %copy.37), channel_id=1, source_target_pairs={{0,112},{16,0},{32,16},{48,32},{64,48},{80,64},{96,80},{112,96},{1... | collective-permute-start | bytes 316808 | tf_op jit(solution)/shard_map/ppermute | solution.py:18
  211.8 4.0 %copy-start.7 = (f32[58,42,138]{2,0,1:T(8,128)S(1)}, f32[58,42,138]{2,0,1:T(8,128)}, u32[]{:S(2)}) copy-start(f32[58,42,138]{2,0,1:T(8,128)} %get-tuple-element.31) | copy-start | bytes 4034020
  225.9 3.0 copy-start.11
  243.1 10.9 %collective-permute-start.24 = (f32[6,40,136]{2,0,1:T(8,128)S(1)}, f32[6,40,136]{2,0,1:T(8,128)S(1)}, u32[]{:S(2)}, u32[]{:S(2)}) collective-permute-start(f32[6,40,136]{2,0,1:T(8,128)S(1)} %get-tuple-element.51), channel_id=1, source_target_pairs={{0,1},{1,2},{2,3},{3,0},{4,5},{5,6},{6,7},{7,4},{8,9},{9,10},{10,1... | collective-permute-start | bytes 391688 | tf_op jit(solution)/shard_map/ppermute | solution.py:18
  243.7 10.4 %collective-permute-start.25 = (f32[6,40,136]{2,0,1:T(8,128)S(1)}, f32[6,40,136]{2,0,1:T(8,128)S(1)}, u32[]{:S(2)}, u32[]{:S(2)}) collective-permute-start(f32[6,40,136]{2,0,1:T(8,128)S(1)} %get-tuple-element.52), channel_id=1, source_target_pairs={{0,3},{1,0},{2,1},{3,2},{4,7},{5,4},{6,5},{7,6},{8,11},{9,8},{10,9... | collective-permute-start | bytes 391688 | tf_op jit(solution)/shard_map/ppermute | solution.py:18
  254.3 10.3 %collective-permute-start.26 = (f32[52,6,136]{2,0,1:T(8,128)S(1)}, f32[52,6,136]{2,0,1:T(8,128)S(1)}, u32[]{:S(2)}, u32[]{:S(2)}) collective-permute-start(f32[52,6,136]{2,0,1:T(8,128)S(1)} %get-tuple-element.49), channel_id=1, source_target_pairs={{0,4},{4,8},{8,12},{12,0},{1,5},{5,9},{9,13},{13,1},{2,6},{6,10},{... | collective-permute-start | bytes 509192 | tf_op jit(solution)/shard_map/ppermute | solution.py:18
  254.4 10.2 %collective-permute-start.27 = (f32[52,6,136]{2,0,1:T(8,128)S(1)}, f32[52,6,136]{2,0,1:T(8,128)S(1)}, u32[]{:S(2)}, u32[]{:S(2)}) collective-permute-start(f32[52,6,136]{2,0,1:T(8,128)S(1)} %get-tuple-element.50), channel_id=1, source_target_pairs={{0,12},{4,0},{8,4},{12,8},{1,13},{5,1},{9,5},{13,9},{2,14},{6,2},{... | collective-permute-start | bytes 509192 | tf_op jit(solution)/shard_map/ppermute | solution.py:18
  264.8 1.4 copy-start.9
  269.5 8.9 %collective-permute-start.28 = (f32[52,36,6]{0,1,2:T(8,128)S(1)}, f32[52,36,6]{0,1,2:T(8,128)S(1)}, u32[]{:S(2)}, u32[]{:S(2)}) collective-permute-start(f32[52,36,6]{0,1,2:T(8,128)S(1)} %copy.40), channel_id=1, source_target_pairs={{0,16},{16,32},{32,48},{48,64},{64,80},{80,96},{96,112},{112,0},{1... | collective-permute-start | bytes 134792 | tf_op jit(solution)/shard_map/ppermute | solution.py:18
  273.5 7.5 %collective-permute-start.29 = (f32[52,36,6]{0,1,2:T(8,128)S(1)}, f32[52,36,6]{0,1,2:T(8,128)S(1)}, u32[]{:S(2)}, u32[]{:S(2)}) collective-permute-start(f32[52,36,6]{0,1,2:T(8,128)S(1)} %copy.42), channel_id=1, source_target_pairs={{0,112},{16,0},{32,16},{48,32},{64,48},{80,64},{96,80},{112,96},{1... | collective-permute-start | bytes 134792 | tf_op jit(solution)/shard_map/ppermute | solution.py:18
  282.4 3.4 copy-start.8
  285.8 3.7 %copy-start.1 = (f32[52,36,132]{2,0,1:T(8,128)}, f32[52,36,132]{2,0,1:T(8,128)S(1)}, u32[]{:S(2)}) copy-start(f32[52,36,132]{2,0,1:T(8,128)S(1)} %fusion.54) | copy-start | bytes 2965252
  285.9 3.7 %copy-start.3 = (f32[48,32,128]{2,1,0:T(8,128)S(1)}, f32[48,32,128]{2,1,0:T(8,128)}, u32[]{:S(2)}) copy-start(f32[48,32,128]{2,1,0:T(8,128)} %param.2) | copy-start | bytes 2359300
  301.8 5.1 %collective-permute-start.30 = (f32[9]{0:T(128)S(1)}, f32[9]{0:T(128)S(1)}, u32[]{:S(2)}, u32[]{:S(2)}) collective-permute-start(f32[9]{0:T(128)S(1)} %stack.39), channel_id=1, source_target_pairs={{0,16},{16,0},{32,48},{48,32},{64,80},{80,64},{96,112},{112,96},{1... | collective-permute-start | bytes 116 | tf_op jit(solution)/shard_map/ppermute | solution.py:109
  306.9 3.5 %collective-permute-start.31 = (f32[9]{0:T(128)S(1)}, f32[9]{0:T(128)S(1)}, u32[]{:S(2)}, u32[]{:S(2)}) collective-permute-start(f32[9]{0:T(128)S(1)} %add.592), channel_id=1, source_target_pairs={{0,32},{16,48},{32,0},{48,16},{64,96},{80,112},{96,64},{112,80},{1... | collective-permute-start | bytes 116 | tf_op jit(solution)/shard_map/ppermute | solution.py:109
  310.4 5.0 %collective-permute-start.32 = (f32[9]{0:T(128)S(1)}, f32[9]{0:T(128)S(1)}, u32[]{:S(2)}, u32[]{:S(2)}) collective-permute-start(f32[9]{0:T(128)S(1)} %add.593), channel_id=1, source_target_pairs={{0,64},{16,80},{32,96},{48,112},{64,0},{80,16},{96,32},{112,48},{1... | collective-permute-start | bytes 116 | tf_op jit(solution)/shard_map/ppermute | solution.py:109
  315.5 1.1 collective-permute-start.33
  316.6 3.5 %collective-permute-start.34 = (f32[9]{0:T(128)S(1)}, f32[9]{0:T(128)S(1)}, u32[]{:S(2)}, u32[]{:S(2)}) collective-permute-start(f32[9]{0:T(128)S(1)} %add.595), channel_id=1, source_target_pairs={{0,8},{4,12},{8,0},{12,4},{1,9},{5,13},{9,1},{13,5},{2,10},{6,14},... | collective-permute-start | bytes 116 | tf_op jit(solution)/shard_map/ppermute | solution.py:109
  320.2 3.5 %collective-permute-start.35 = (f32[9]{0:T(128)S(1)}, f32[9]{0:T(128)S(1)}, u32[]{:S(2)}, u32[]{:S(2)}) collective-permute-start(f32[9]{0:T(128)S(1)} %add.596), channel_id=1, source_target_pairs={{0,1},{1,0},{2,3},{3,2},{4,5},{5,4},{6,7},{7,6},{8,9},{9,8},{10,11... | collective-permute-start | bytes 116 | tf_op jit(solution)/shard_map/ppermute | solution.py:109
  323.7 5.0 %collective-permute-start.36 = (f32[9]{0:T(128)S(1)}, f32[9]{0:T(128)S(1)}, u32[]{:S(2)}, u32[]{:S(2)}) collective-permute-start(f32[9]{0:T(128)S(1)} %add.597), channel_id=1, source_target_pairs={{0,2},{1,3},{2,0},{3,1},{4,6},{5,7},{6,4},{7,5},{8,10},{9,11},{10,... | collective-permute-start | bytes 116 | tf_op jit(solution)/shard_map/ppermute | solution.py:109
  344.8 2.9 copy-start.4
  344.9 2.9 copy-start.24
